TPU v7x, 128 devices: a whole 4x4x4 slice. The times are simulated.
128 devices in a mesh: lon: 8 (over z_lo, x), lat: 16 (over z_hi, y, core).
Axes of the slice: x: 4, y: 4, z: 4 (z_hi: 2, z_lo: 2; z = z_hi * 2 + z_lo), core: 2. Of those that a mesh axis runs over, the one named last changes fastest.
Arguments:
- tokens: float32 [2, 240, 800, 512], P(None, 'lat', 'lon'), may hold values from -6 to 6
- ln_gain: float32 [512], replicated, may hold values from 0.1 to 1.9
- ln_shift: float32 [512], replicated, may hold values from -3 to 3
- w_qkv: float32 [512, 1536], replicated, may hold values from -0.25 to 0.25
- w_out: float32 [512, 512], replicated, may hold values from -0.25 to 0.25
- region_ids: int32 [240], replicated, may hold values from 0 to 29, never falling along the last dimension, each value on 1 to 16 neighbouring positions
- position_bias: float32 [48, 16, 100, 100], P('lat'), may hold values from -4 to 400
Outputs:
- updated: float32 [2, 240, 800, 512], P(None, 'lat', 'lon')
Inputs may be any that keep to these rules, and one draw needn't show every extreme that they name: `region_ids`: ids never fall along latitude; each id covers 1 to 16 consecutive rows, one exactly 16.
All inputs are finite; a program needn't handle non-finite values.
Results may differ from a plain program's by a relative error of at most 0.0003.
Values sent between devices are 32-bit elements; how exact they have to be, the bound alone decides.
No kernel may reach another device: no remote copies, remote signals or barrier semaphores. Data moves between devices by JAX's collectives and lax.ppermute only.
A program may use at most 192 MiB of HBM per device.

v0:
```python
import functools
import math

import jax
import jax.numpy as jnp
from jax import lax
from jax.experimental import pallas as pl
from jax.experimental.pallas import tpu as pltpu
from jax.sharding import PartitionSpec as P

D = 512
HEADS = 16
WLON = 10
WLAT = 5
HALF_LAT = WLAT // 2
HALF_LON = WLON // 2
ROWS = 15
COLS = 100
BANDS = ROWS // WLAT
ACROSS = COLS // WLON
SUB = 8
CELLS = WLAT * WLON
CELL_PAD = 56
TOK_PAD = 2 * CELL_PAD
SLAB = CELL_PAD * SUB
S_COLS = COLS - HALF_LON
NEG = -1e30
LOG2E = math.log2(math.e)
QSCALE = LOG2E / math.sqrt(D // HEADS)
BF = jnp.bfloat16
F32 = jnp.float32


def hi_lo(x):
    hi = x.astype(BF)
    lo = (x - hi.astype(F32)).astype(BF)
    return hi, lo


def pieces(band, win):
    out = []
    for i in range(WLAT):
        row = WLAT * band + HALF_LAT + i
        col = WLON * win + HALF_LON
        wide = min(WLON, COLS - col)
        south = row >= ROWS
        if south:
            out.append((i * WLON, "s", (row - ROWS) * S_COLS + col - HALF_LON, wide))
        else:
            out.append((i * WLON, "t", row * COLS + col, wide))
        if wide < WLON:
            if south:
                out.append((i * WLON + wide, "c", (row - ROWS) * HALF_LON, WLON - wide))
            else:
                out.append((i * WLON + wide, "e", (row - HALF_LAT) * HALF_LON, WLON - wide))
    return out


def dot(a, b):
    return lax.dot_general(a, b, (((1,), (0,)), ((), ())), preferred_element_type=F32)


def dot_t(a, b):
    return lax.dot_general(a, b, (((1,), (1,)), ((), ())), preferred_element_type=F32)


def group_kernel(runs, halo, aliased, *refs):
    refs = list(refs)
    ids_ref, tok_hbm = refs[:2]
    del refs[:2]
    srcs = {"t": tok_hbm}
    if halo:
        srcs.update(zip("sec", refs[:3]))
        del refs[:3]
    gain_ref, shift_ref, wqkv_hbm, wout_hbm, bias_hbm = refs[:5]
    del refs[:5]
    if aliased:
        del refs[0]
    dsts = {"t": refs.pop(0)}
    if halo:
        dsts.update(zip("sec", refs[:3]))
        del refs[:3]
    (tok, stage_q, stage_o, bias_v, wq, wo, xcat, qkv, hcat, biasm,
     sem_tok, sem_w, sem_b, sem_out) = refs

    wins = [(b, w) for b, ws in runs for w in ws]
    nw = len(wins)
    rows_all = nw * TOK_PAD

    def move(i, srcs_or_dsts, into, sem):
        band, win = wins[i]
        for cell, name, start, count in pieces(band, win):
            here = tok.at[pl.ds(i * SLAB + cell * SUB, count * SUB)]
            there = srcs_or_dsts[name].at[pl.ds(start * SUB, count * SUB)]
            if into:
                pltpu.make_async_copy(there, here, sem).start()
            else:
                pltpu.make_async_copy(here, there, sem).start()

    for i in range(nw):
        move(i, srcs, True, sem_tok.at[i])
    copy_q = pltpu.make_async_copy(wqkv_hbm, stage_q, sem_w.at[0])
    copy_o = pltpu.make_async_copy(wout_hbm, stage_o, sem_w.at[1])
    copy_q.start()
    copies_b = []
    for j, (b, _) in enumerate(runs):
        c = pltpu.make_async_copy(
            bias_hbm.at[pl.ds(b * 1600, 1600)], bias_v.at[j, pl.ds(0, 1600)], sem_b.at[j])
        c.start()
        copies_b.append(c)
    copy_o.start()

    gain = gain_ref[...].reshape(1, D)
    shift = shift_ref[...].reshape(1, D)
    pad_rows = jnp.zeros(((CELL_PAD - CELLS) * SUB, 128), F32)

    def norm_window(i, _):
        base = pl.multiple_of(i * SLAB, SLAB)
        pltpu.make_async_copy(
            tok_hbm.at[pl.ds(0, CELLS * SUB)], tok.at[pl.ds(base, CELLS * SUB)], sem_tok.at[i]).wait()
        tok[pl.ds(base + CELLS * SUB, (CELL_PAD - CELLS) * SUB), :] = pad_rows
        parts = [
            jnp.concatenate(
                [tok[pl.ds(base + g * 2 + lev, CELL_PAD, stride=SUB), :] for lev in range(2)], axis=0)
            for g in range(4)
        ]
        center = jnp.sum(parts[0] + parts[1] + parts[2] + parts[3], axis=1, keepdims=True) * (1.0 / D)
        parts = [p - center for p in parts]
        sq = [p * p for p in parts]
        spread = jnp.sum(sq[0] + sq[1] + sq[2] + sq[3], axis=1, keepdims=True) * (1.0 / D)
        scale = lax.rsqrt(spread + 1e-05)
        r = pl.ds(pl.multiple_of(i * TOK_PAD, TOK_PAD), TOK_PAD)
        for g in range(4):
            cols = slice(g * 128, (g + 1) * 128)
            y = parts[g] * scale * gain[:, cols] + shift[:, cols]
            hi, lo = hi_lo(y)
            xcat[r, g * 128:(g + 1) * 128] = hi
            xcat[r, D + g * 128:D + (g + 1) * 128] = lo
        return 0

    lax.fori_loop(0, nw, norm_window, 0)

    copy_q.wait()

    def split_q(i, _):
        r = pl.ds(pl.multiple_of(i * 16, 16), 16)
        for part in range(3):
            x = stage_q[r, part * D:(part + 1) * D]
            if part == 0:
                x = x * QSCALE
            hi, lo = hi_lo(x)
            wq[r, part * D:(part + 1) * D] = hi
            wq[pl.ds(pl.multiple_of(i * 16 + D, 16), 16), part * D:(part + 1) * D] = hi
            wq[pl.ds(pl.multiple_of(i * 16 + 2 * D, 16), 16), part * D:(part + 1) * D] = lo
        return 0

    lax.fori_loop(0, D // 16, split_q, 0)
    copy_o.wait()

    def split_o(i, _):
        r = pl.ds(pl.multiple_of(i * 16, 16), 16)
        hi, lo = hi_lo(stage_o[r, :])
        wo[r, :] = hi
        wo[pl.ds(pl.multiple_of(i * 16 + D, 16), 16), :] = hi
        wo[pl.ds(pl.multiple_of(i * 16 + 2 * D, 16), 16), :] = lo
        return 0

    lax.fori_loop(0, D // 16, split_o, 0)

    for t in range(6):
        cols = slice(t * 256, (t + 1) * 256)
        qkv[:, cols] = dot(xcat[...], wq[0:2 * D, cols]) + dot(xcat[:, 0:D], wq[2 * D:3 * D, cols])

    lat_at = lax.axis_index("lat")
    q_at = lax.broadcasted_iota(jnp.int32, (TOK_PAD, 128), 0)
    k_at = lax.broadcasted_iota(jnp.int32, (TOK_PAD, 128), 1)
    q_cell = jnp.where(q_at >= CELL_PAD, q_at - CELL_PAD, q_at)
    k_cell = jnp.where(k_at >= CELL_PAD, k_at - CELL_PAD, k_at)
    k_real = (k_cell < CELLS)
    for j, (b, _) in enumerate(runs):
        copies_b[j].wait()
        bias_v[j, 1600:, :] = jnp.zeros((bias_v.shape[1] - 1600, 100), F32)
        idq = jnp.zeros((TOK_PAD, 128), jnp.int32)
        idk = jnp.zeros((TOK_PAD, 128), jnp.int32)
        for i in range(WLAT):
            at = lat_at * ROWS + b * WLAT + i + HALF_LAT
            one = ids_ref[jnp.where(at >= 240, at - 240, at)]
            idq = jnp.where(q_cell >= i * WLON, one, idq)
            idk = jnp.where(k_cell >= i * WLON, one, idk)
        ok = jnp.logical_and(idq == idk, k_real)
        early = k_at < CELL_PAD
        for h in range(HEADS):
            raw = jnp.concatenate(
                [bias_v[j, pl.ds(h, CELL_PAD, stride=HEADS), :],
                 bias_v[j, pl.ds(h + CELLS * HEADS, CELL_PAD, stride=HEADS), :]], axis=0) * LOG2E
            raw = jnp.concatenate([raw, jnp.zeros((TOK_PAD, 28), F32)], axis=1)
            moved = pltpu.roll(raw, CELL_PAD - CELLS, 1)
            biasm[j, h] = jnp.where(ok, jnp.where(early, raw, moved), NEG)

    lane = lax.broadcasted_iota(jnp.int32, (TOK_PAD, 128), 1)
    low_half = lane < 64
    zeros16 = jnp.zeros((16, 256), BF)
    ends = []
    total = 0
    for _, ws in runs:
        total += len(ws)
        ends.append(total)

    def swap(x):
        return jnp.concatenate([x[:, 64:], x[:, :64]], axis=1)

    def attend_window(i, _):
        r = pl.ds(pl.multiple_of(i * TOK_PAD, TOK_PAD), TOK_PAD)
        slot = 0
        for e in ends[:-1]:
            slot = slot + jnp.where(i >= e, 1, 0)
        for g in range(4):
            q = qkv[r, g * 128:(g + 1) * 128]
            k = qkv[r, D + g * 128:D + (g + 1) * 128]
            v = qkv[r, 2 * D + g * 128:2 * D + (g + 1) * 128]
            qh = q.astype(BF).astype(F32)
            ql = q - qh
            rql = pltpu.roll(ql, 64, 1)
            kh = k.astype(BF).astype(F32)
            kl = k - kh
            rkh = pltpu.roll(kh, 64, 1)
            rkl = pltpu.roll(kl, 64, 1)
            vh, vl = hi_lo(v)
            vh = vh.astype(F32)
            vl = vl.astype(F32)
            sides_q = (jnp.where(low_half, qh, rql).astype(BF), jnp.where(low_half, rql, qh).astype(BF))
            sides_kh = (jnp.where(low_half, kh, rkh), jnp.where(low_half, rkh, kh))
            sides_kl = (jnp.where(low_half, kl, rkl), jnp.where(low_half, rkl, kl))
            his, los, inv, rhs = [], [], [], []
            for s in range(2):
                lhs = jnp.concatenate([sides_q[s], sides_q[s]], axis=1)
                keys = []
                for t in range(2):
                    own = jnp.logical_and((lane & 63) >= 32 * t, (lane & 63) < 32 * (t + 1))
                    part = jnp.concatenate(
                        [jnp.where(own, sides_kh[s], 0.0).astype(BF),
                         jnp.where(own, sides_kl[s], 0.0).astype(BF)], axis=1)
                    keys += [part, zeros16]
                scores = dot_t(lhs, jnp.concatenate(keys, axis=0))
                for t in range(2):
                    h = g * 4 + s * 2 + t
                    x = scores[:, t * 128:(t + 1) * 128] + biasm[slot, h]
                    x = jnp.exp2(x - jnp.max(x, axis=1, keepdims=True))
                    inv.append(1.0 / jnp.sum(x, axis=1, keepdims=True))
                    hi, lo = hi_lo(x)
                    his.append(hi)
                    los.append(lo)
                    own = jnp.logical_and(lane >= 32 * (2 * s + t), lane < 32 * (2 * s + t + 1))
                    part = jnp.concatenate(
                        [jnp.where(own, vh, 0.0).astype(BF), jnp.where(own, vl, 0.0).astype(BF)], axis=1)
                    rhs += [part, zeros16]
            lhs = jnp.concatenate([jnp.concatenate(his, axis=1), jnp.concatenate(los, axis=1)], axis=0)
            both = dot(lhs, jnp.concatenate(rhs, axis=0))
            both = both[:TOK_PAD] + both[TOK_PAD:]
            out = both[:, :128] + both[:, 128:]
            scale = jnp.where(
                lane < 64, jnp.where(lane < 32, inv[0], inv[1]), jnp.where(lane < 96, inv[2], inv[3]))
            hi, lo = hi_lo(out * scale)
            hcat[r, g * 128:(g + 1) * 128] = hi
            hcat[r, D + g * 128:D + (g + 1) * 128] = lo
        return 0

    lax.fori_loop(0, nw, attend_window, 0)

    for t in range(2):
        cols = slice(t * 256, (t + 1) * 256)
        qkv[:, cols] = dot(hcat[...], wo[0:2 * D, cols]) + dot(hcat[:, 0:D], wo[2 * D:3 * D, cols])

    def add_window(i, _):
        base = pl.multiple_of(i * SLAB, SLAB)
        for lev in range(2):
            r = pl.ds(pl.multiple_of(i * TOK_PAD + lev * CELL_PAD, CELL_PAD), CELL_PAD)
            for g in range(4):
                at = pl.ds(base + g * 2 + lev, CELL_PAD, stride=SUB)
                tok[at, :] = tok[at, :] + qkv[r, g * 128:(g + 1) * 128]
        return 0

    lax.fori_loop(0, nw, add_window, 0)
    for i in range(nw):
        move(i, dsts, False, sem_out.at[i])
    for i in range(nw):
        pltpu.make_async_copy(
            tok.at[pl.ds(i * SLAB, CELLS * SUB)], tok_hbm.at[pl.ds(0, CELLS * SUB)], sem_out.at[i]).wait()


def group_call(runs, ids, tok, halos, gain, shift, w_qkv, w_out, bias, out_so_far, name):
    nw = sum(len(ws) for _, ws in runs)
    nb = len(runs)
    halo = halos is not None
    aliased = out_so_far is not None
    any_spec = pl.BlockSpec(memory_space=pl.ANY)
    vmem_spec = pl.BlockSpec(memory_space=pltpu.VMEM)
    smem_spec = pl.BlockSpec(memory_space=pltpu.SMEM)
    args = [ids, tok]
    specs = [smem_spec, any_spec]
    if halo:
        args += list(halos)
        specs += [any_spec] * 3
    args += [gain, shift, w_qkv, w_out, bias]
    specs += [vmem_spec, vmem_spec, any_spec, any_spec, any_spec]
    aliases = {}
    if aliased:
        aliases = {len(args): 0}
        args.append(out_so_far)
        specs.append(any_spec)
    out_shapes = [jax.ShapeDtypeStruct(tok.shape, F32)]
    if halo:
        out_shapes += [jax.ShapeDtypeStruct(h.shape, F32) for h in halos]
    rows_all = nw * TOK_PAD
    return pl.pallas_call(
        functools.partial(group_kernel, runs, halo, aliased),
        out_shape=out_shapes,
        in_specs=specs,
        out_specs=[any_spec] * len(out_shapes),
        input_output_aliases=aliases,
        scratch_shapes=[
            pltpu.VMEM((nw * SLAB, 128), F32),
            pltpu.VMEM((D, 3 * D), F32),
            pltpu.VMEM((D, D), F32),
            pltpu.VMEM((nb, 1712, 100), F32),
            pltpu.VMEM((3 * D, 3 * D), BF),
            pltpu.VMEM((3 * D, D), BF),
            pltpu.VMEM((rows_all, 2 * D), BF),
            pltpu.VMEM((rows_all, 3 * D), F32),
            pltpu.VMEM((rows_all, 2 * D), BF),
            pltpu.VMEM((nb, HEADS, TOK_PAD, 128), F32),
            pltpu.SemaphoreType.DMA((nw,)),
            pltpu.SemaphoreType.DMA((2,)),
            pltpu.SemaphoreType.DMA((nb,)),
            pltpu.SemaphoreType.DMA((nw,)),
        ],
        compiler_params=pltpu.CompilerParams(vmem_limit_bytes=56 << 20),
        cost_estimate=pl.CostEstimate(
            flops=nw * 10**9, bytes_accessed=8 << 20, transcendentals=nw * 200000),
        name=name,
    )(*args)


def merge_kernel(s_ref, e_ref, c_ref, _, out_ref, sem):
    copies = []
    for row in range(HALF_LAT):
        copies.append((s_ref, row * S_COLS, row * COLS + HALF_LON, S_COLS))
        copies.append((c_ref, row * HALF_LON, row * COLS, HALF_LON))
    for row in range(HALF_LAT, ROWS):
        copies.append((e_ref, (row - HALF_LAT) * HALF_LON, row * COLS, HALF_LON))
    started = []
    for n, (src, start, place, count) in enumerate(copies):
        c = pltpu.make_async_copy(
            src.at[pl.ds(start * SUB, count * SUB)], out_ref.at[pl.ds(place * SUB, count * SUB)], sem.at[n])
        c.start()
        started.append(c)
    for c in started:
        c.wait()


def merge_call(s, e, c, out_so_far):
    any_spec = pl.BlockSpec(memory_space=pl.ANY)
    return pl.pallas_call(
        merge_kernel,
        out_shape=jax.ShapeDtypeStruct(out_so_far.shape, F32),
        in_specs=[pl.BlockSpec(memory_space=pltpu.VMEM)] * 3 + [any_spec],
        out_specs=any_spec,
        input_output_aliases={3: 0},
        scratch_shapes=[pltpu.SemaphoreType.DMA((HALF_LAT + ROWS,))],
        name="merge",
    )(s, e, c, out_so_far)


def shift_pairs(dlon, dlat):
    n_lon, n_lat = lax.axis_size("lon"), lax.axis_size("lat")
    pairs = []
    for lon in range(n_lon):
        for lat in range(n_lat):
            to = ((lon + dlon) % n_lon) * n_lat + (lat + dlat) % n_lat
            pairs.append((lon * n_lat + lat, to))
    return pairs


def send(value, dlon, dlat):
    return lax.ppermute(value, ("lon", "lat"), shift_pairs(dlon, dlat))


def body(tokens, ln_gain, ln_shift, w_qkv, w_out, region_ids, position_bias):
    tok = tokens.transpose(1, 2, 0, 3).reshape(ROWS, COLS, 2, 4, 128)
    tok = tok.transpose(0, 1, 3, 2, 4).reshape(ROWS, COLS * SUB, 128)
    bias = position_bias.transpose(0, 2, 1, 3).reshape(BANDS * 100 * HEADS, 100)
    edge = HALF_LON * SUB
    s = send(tok[:HALF_LAT, edge:].reshape(-1, 128), 0, -1)
    e = send(tok[HALF_LAT:, :edge].reshape(-1, 128), -1, 0)
    c = send(tok[:HALF_LAT, :edge].reshape(-1, 128), -1, -1)
    tok = tok.reshape(-1, 128)
    common = (ln_gain, ln_shift, w_qkv, w_out, bias)
    inner = tuple(range(ACROSS - 1))
    (out,) = group_call(((0, inner),), region_ids, tok, None, *common, None, "band0")
    out, s, e, c = group_call(
        ((2, tuple(range(ACROSS))), (0, (ACROSS - 1,)), (1, (ACROSS - 1,))),
        region_ids, tok, (s, e, c), *common, out, "rim")
    s = send(s, 0, 1)
    e = send(e, 1, 0)
    c = send(c, 1, 1)
    (out,) = group_call(((1, inner),), region_ids, tok, None, *common, out, "band1")
    out = merge_call(s, e, c, out)
    out = out.reshape(ROWS, COLS, 4, 2, 128).transpose(0, 1, 3, 2, 4).reshape(ROWS, COLS, 2, D)
    return out.transpose(2, 0, 1, 3)


def solution(mesh):
    in_specs = (P(None, "lat", "lon", None), P(), P(), P(), P(), P(), P("lat", None, None, None))
    out_specs = P(None, "lat", "lon", None)
    return jax.shard_map(body, mesh=mesh, in_specs=in_specs, out_specs=out_specs, check_vma=False)
```

profile of v0, /device:TPU:0, one launch (start us, length us, event | category | flops | bytes accessed | tf_op | source)
XLA Modules:
  0.0 103.3 jit_solution(14524891113335686942)
XLA Ops:
  0.0 0.8 slice.14
  0.8 8.2 %collective-permute-start.2 = (f32[80,128]{1,0:T(8,128)S(1)}, f32[80,128]{1,0:T(8,128)S(1)}, u32[]{:S(2)}, u32[]{:S(2)}) collective-permute-start(f32[80,128]{1,0:T(8,128)S(1)} %bitcast.30), channel_id=1, source_target_pairs={{0,127},{1,112},{2,113},{3,114},{4,115},{5,116},{6,117},{7,118},{8... | collective-permute-start | bytes 122888 | tf_op jit(solution)/shard_map/ppermute | solution.py:385
  9.0 1.0 slice.13
  10.0 1.2 %collective-permute-start.1 = (f32[520,128]{1,0:T(8,128)S(1)}, f32[520,128]{1,0:T(8,128)S(1)}, u32[]{:S(2)}, u32[]{:S(2)}) collective-permute-start(f32[520,128]{1,0:T(8,128)S(1)} %bitcast.23), channel_id=1, source_target_pairs={{0,112},{1,113},{2,114},{3,115},{4,116},{5,117},{6,118},{7,119},{8... | collective-permute-start | bytes 798728 | tf_op jit(solution)/shard_map/ppermute | solution.py:385
  11.2 1.2 %slice.12 = f32[2,760,128]{2,1,0:T(8,128)S(1)} slice(f32[15,800,128]{2,1,0:T(8,128)} %bitcast.26), slice={[0:2], [40:800], [0:128]} | slice | bytes 1556480 | tf_op jit(solution)/shard_map/slice | solution.py:393
  12.3 1.2 %collective-permute-start = (f32[1520,128]{1,0:T(8,128)S(1)}, f32[1520,128]{1,0:T(8,128)S(1)}, u32[]{:S(2)}, u32[]{:S(2)}) collective-permute-start(f32[1520,128]{1,0:T(8,128)S(1)} %bitcast.22), channel_id=1, source_target_pairs={{0,15},{1,0},{2,1},{3,2},{4,3},{5,4},{6,5},{7,6},{8,7},{9,8},{10,9... | collective-permute-start | bytes 2334728 | tf_op jit(solution)/shard_map/ppermute | solution.py:385
  13.6 24.7 %band0.1.refs_10_ = f32[12000,128]{1,0:T(8,128)} custom-call(s32[240]{0:T(256)} %refs_0_.5, f32[12000,128]{1,0:T(8,128)} %bitcast.27, f32[512]{0:T(512)} %refs_2_.3, f32[512]{0:T(512)} %refs_3_.3, f32[512,1536]{1,0:T(8,128)} %refs_4_.3, f32[512,512]{1,0:T(8,128)} %refs_5_.5, f32[4800,100]{1,0:T(8,128)} %bitcast.31), custom_call_target="tpu_custom_call" | custom-call | flops 8999999488 | bytes 8388608 | tf_op jit(solution)/shard_map/band0/pallas_call | solution.py:315
  38.3 0.0 collective-permute-done.2.refs_4_
  38.3 0.0 collective-permute-done.1.refs_3_
  38.4 0.0 collective-permute-done.refs_2_
  38.4 0.6 copy-done.5
  38.9 0.1 copy-done.4
  39.1 0.9 copy-done.3
  40.0 33.1 %rim.1 = (f32[12000,128]{1,0:T(8,128)}, f32[1520,128]{1,0:T(8,128)}, f32[520,128]{1,0:T(8,128)}, f32[80,128]{1,0:T(8,128)}) custom-call(s32[240]{0:T(256)} %refs_0_.5, f32[12000,128]{1,0:T(8,128)} %bitcast.28, f32[1520,128]{1,0:T(8,128)} %copy-done.3, f32[520,128]{1,0:T(8,128)} %copy-done.4, f32[80,128]{1,0:T(8,128)} %copy-done.5, ...), custom_call_target="tpu_custom_call", output_to_operand_aliasing={{0}: (10, {})} | custom-call | flops 12000000000 | bytes 8388608 | tf_op jit(solution)/shard_map/rim/pallas_call | solution.py:315
  73.1 0.1 collective-permute-start.5
  73.2 1.3 %collective-permute-start.4 = (f32[520,128]{1,0:T(8,128)}, f32[520,128]{1,0:T(8,128)S(1)}, u32[]{:S(2)}, u32[]{:S(2)}) collective-permute-start(f32[520,128]{1,0:T(8,128)} %get-tuple-element.10), channel_id=1, source_target_pairs={{0,16},{1,17},{2,18},{3,19},{4,20},{5,21},{6,22},{7,23},{8,24},{9,... | collective-permute-start | bytes 798728 | tf_op jit(solution)/shard_map/ppermute | solution.py:385
  74.4 0.0 collective-permute-start.3
  74.4 24.7 %band1.1._ = f32[12000,128]{1,0:T(8,128)} custom-call(s32[240]{0:T(256)} %refs_0_.5, f32[12000,128]{1,0:T(8,128)} %bitcast.29, f32[512]{0:T(512)} %refs_2_.3, f32[512]{0:T(512)} %refs_3_.3, f32[512,1536]{1,0:T(8,128)} %refs_4_.3, f32[512,512]{1,0:T(8,128)} %refs_5_.5, f32[4800,100]{1,0:T(8,128)} %bitcast.33, ...), custom_call_target="tpu_custom_call", output_to_operand_aliasing={{}: (7, {})} | custom-call | flops 8999999488 | bytes 8388608 | tf_op jit(solution)/shard_map/band1/pallas_call | solution.py:315
  99.2 0.0 collective-permute-done.5.c_ref
  99.2 0.0 collective-permute-done.4.e_ref
  99.2 0.6 copy-done.2
  99.8 0.1 copy-done.1
  99.9 0.9 copy-done
  100.8 2.3 %merge.1 = f32[12000,128]{1,0:T(8,128)} custom-call(f32[1520,128]{1,0:T(8,128)} %copy-done, f32[520,128]{1,0:T(8,128)} %copy-done.1, f32[80,128]{1,0:T(8,128)} %copy-done.2, f32[12000,128]{1,0:T(8,128)} %band1.1._), custom_call_target="tpu_custom_call", output_to_operand_aliasing={{}: (3, {})} | custom-call | tf_op jit(solution)/shard_map/merge/pallas_call | solution.py:363
  (7 shorter events, 0.0 us)
Async XLA Ops:
  0.8 37.5 %collective-permute-start.2 = (f32[80,128]{1,0:T(8,128)S(1)}, f32[80,128]{1,0:T(8,128)S(1)}, u32[]{:S(2)}, u32[]{:S(2)}) collective-permute-start(f32[80,128]{1,0:T(8,128)S(1)} %bitcast.30), channel_id=1, source_target_pairs={{0,127},{1,112},{2,113},{3,114},{4,115},{5,116},{6,117},{7,118},{8... | collective-permute-start | bytes 122888 | tf_op jit(solution)/shard_map/ppermute | solution.py:385
  10.0 28.4 %collective-permute-start.1 = (f32[520,128]{1,0:T(8,128)S(1)}, f32[520,128]{1,0:T(8,128)S(1)}, u32[]{:S(2)}, u32[]{:S(2)}) collective-permute-start(f32[520,128]{1,0:T(8,128)S(1)} %bitcast.23), channel_id=1, source_target_pairs={{0,112},{1,113},{2,114},{3,115},{4,116},{5,117},{6,118},{7,119},{8... | collective-permute-start | bytes 798728 | tf_op jit(solution)/shard_map/ppermute | solution.py:385
  12.3 26.0 %collective-permute-start = (f32[1520,128]{1,0:T(8,128)S(1)}, f32[1520,128]{1,0:T(8,128)S(1)}, u32[]{:S(2)}, u32[]{:S(2)}) collective-permute-start(f32[1520,128]{1,0:T(8,128)S(1)} %bitcast.22), channel_id=1, source_target_pairs={{0,15},{1,0},{2,1},{3,2},{4,3},{5,4},{6,5},{7,6},{8,7},{9,8},{10,9... | collective-permute-start | bytes 2334728 | tf_op jit(solution)/shard_map/ppermute | solution.py:385
  38.3 0.6 copy-start.5
  38.4 0.7 copy-start.4
  39.1 0.9 copy-start.3
  73.1 26.1 %collective-permute-start.5 = (f32[80,128]{1,0:T(8,128)}, f32[80,128]{1,0:T(8,128)S(1)}, u32[]{:S(2)}, u32[]{:S(2)}) collective-permute-start(f32[80,128]{1,0:T(8,128)} %get-tuple-element.11), channel_id=1, source_target_pairs={{0,17},{1,18},{2,19},{3,20},{4,21},{5,22},{6,23},{7,24},{8,25},{9,... | collective-permute-start | bytes 122888 | tf_op jit(solution)/shard_map/ppermute | solution.py:385
  73.2 26.0 %collective-permute-start.4 = (f32[520,128]{1,0:T(8,128)}, f32[520,128]{1,0:T(8,128)S(1)}, u32[]{:S(2)}, u32[]{:S(2)}) collective-permute-start(f32[520,128]{1,0:T(8,128)} %get-tuple-element.10), channel_id=1, source_target_pairs={{0,16},{1,17},{2,18},{3,19},{4,20},{5,21},{6,22},{7,23},{8,24},{9,... | collective-permute-start | bytes 798728 | tf_op jit(solution)/shard_map/ppermute | solution.py:385
  74.4 24.8 %collective-permute-start.3 = (f32[1520,128]{1,0:T(8,128)}, f32[1520,128]{1,0:T(8,128)S(1)}, u32[]{:S(2)}, u32[]{:S(2)}) collective-permute-start(f32[1520,128]{1,0:T(8,128)} %get-tuple-element.9), channel_id=1, source_target_pairs={{0,1},{1,2},{2,3},{3,4},{4,5},{5,6},{6,7},{7,8},{8,9},{9,10},{10,1... | collective-permute-start | bytes 2334728 | tf_op jit(solution)/shard_map/ppermute | solution.py:385
  99.2 0.6 copy-start.2
  99.2 0.7 copy-start.1
  99.9 0.9 copy-start
where the time goes:
time: 104 us; the launch traced here: 103 us
  Pallas kernels  84.9 us (82%)
  starting transfers between devices  12 us (12%)
  local copies, waits for them, and re-layouts  6.13 us (6%)
    pallas_call x3, Pallas kernels, group_call(): pl.pallas_call(functools.partial(group_kernel, runs, halo, aliased), out_...  82.6 us
    ppermute x6, starting transfers between devices, send(): return lax.ppermute(value, ('lon', 'lat'), shift_pairs(dlon, dlat))  12 us
    unnamed x12, local copies, waits for them, and re-layouts  3.19 us
    pallas_call x1, Pallas kernels, merge_call(): pl.pallas_call(merge_kernel, out_shape=jax.ShapeDtypeStruct(out_so_far.sh...  2.32 us
  transfers between devices with their start and end apart: 6, of which 0 were waited for; matrix products, arithmetic and copies ran while one was open for 2% of the time, Pallas kernels for 48%

commit v1 on v0

v1 whole, which is shorter than its diff:
```python
import functools
import math

import jax
import jax.numpy as jnp
from jax import lax
from jax.experimental import pallas as pl
from jax.experimental.pallas import tpu as pltpu
from jax.sharding import PartitionSpec as P

D = 512
HEADS = 16
WLON = 10
WLAT = 5
HALF_LAT = WLAT // 2
HALF_LON = WLON // 2
ROWS = 15
COLS = 100
BANDS = ROWS // WLAT
ACROSS = COLS // WLON
SUB = 8
CELLS = WLAT * WLON
CELL_PAD = 56
TOK_PAD = 2 * CELL_PAD
WIN_ROWS = WLAT + 1
SLAB = WIN_ROWS * WLON * SUB
S_COLS = COLS - HALF_LON
NEG = -1e30
LOG2E = math.log2(math.e)
TILES = 3
QSCALE = LOG2E / math.sqrt(D // HEADS)
BF = jnp.bfloat16
F32 = jnp.float32


def hi_lo(x):
    hi = x.astype(BF)
    lo = (x - hi.astype(F32)).astype(BF)
    return hi, lo


def pieces(band, win):
    top = WLAT * band + HALF_LAT
    col = WLON * win + HALF_LON
    north = min(WLAT, ROWS - top)
    wide = min(WLON, COLS - col)
    out = [(0, 0, "t", top, col, north, wide)]
    if north < WLAT:
        out.append((north, 0, "s", 0, col - HALF_LON, WLAT - north, wide))
    if wide < WLON:
        out.append((0, wide, "e", top - HALF_LAT, 0, north, WLON - wide))
        if north < WLAT:
            out.append((north, wide, "c", 0, 0, WLAT - north, WLON - wide))
    return out


def dot(a, b):
    return lax.dot_general(a, b, (((1,), (0,)), ((), ())), preferred_element_type=F32)


def dot_t(a, b):
    return lax.dot_general(a, b, (((1,), (1,)), ((), ())), preferred_element_type=F32)


def group_kernel(runs, halo, aliased, first, *refs):
    refs = list(refs)
    ids_ref, tok_hbm = refs[:2]
    del refs[:2]
    srcs = {"t": tok_hbm}
    if halo:
        srcs.update(zip("sec", refs[:3]))
        del refs[:3]
    gain_ref, shift_ref, wqkv_hbm, wout_hbm, bias_hbm = refs[:5]
    del refs[:5]
    if aliased:
        del refs[0]
    dsts = {"t": refs.pop(0)}
    if halo:
        dsts.update(zip("sec", refs[:3]))
        del refs[:3]
    if first:
        wq_out, wo_out = refs[:2]
        stage_q, stage_o = refs[-2:]
        refs = refs[2:-2]
    (tok3, bias_v, wq, wo, xcat, qkv, q_t, v_t, hcat, biasm, sem_tok, sem_w, sem_b, sem_out) = refs
    tok = tok3.reshape(tok3.shape[0] * WLON * SUB, 128)

    wins = [(b, w) for b, ws in runs for w in ws]
    nw = len(wins)
    rows_all = nw * TOK_PAD

    def move(i, others, into, sem):
        band, win = wins[i]
        for r0, c0, name, row, col, rows, cols in pieces(band, win):
            here = tok3.at[pl.ds(i * WIN_ROWS + r0, rows), pl.ds(c0 * SUB, cols * SUB)]
            there = others[name].at[pl.ds(row, rows), pl.ds(col * SUB, cols * SUB)]
            if into:
                pltpu.make_async_copy(there, here, sem).start()
            else:
                pltpu.make_async_copy(here, there, sem).start()

    def whole(i, others):
        return others["t"].at[pl.ds(0, WLAT), pl.ds(0, WLON * SUB)], tok3.at[
            pl.ds(i * WIN_ROWS, WLAT), pl.ds(0, WLON * SUB)]

    land_q, land_o = (stage_q, stage_o) if first else (wq, wo)
    copies_q = []
    for t in range(TILES):
        cols = pl.ds(t * D, D)
        copies_q.append(pltpu.make_async_copy(wqkv_hbm.at[:, cols], land_q.at[:, cols], sem_w.at[t]))
    copy_o = pltpu.make_async_copy(wout_hbm, land_o, sem_w.at[TILES])
    copies_b = []
    for j, (b, _) in enumerate(runs):
        copies_b.append(pltpu.make_async_copy(
            bias_hbm.at[pl.ds(b * 1600, 1600)], bias_v.at[j, pl.ds(0, 1600)], sem_b.at[j]))
    for i in range(nw):
        move(i, srcs, True, sem_tok.at[i])
    for c in [copies_q[2], copies_q[0]] + copies_b + [copies_q[1], copy_o]:
        c.start()

    gain = gain_ref[...].reshape(1, D)
    shift = shift_ref[...].reshape(1, D)
    pad_rows = jnp.zeros(((CELL_PAD - CELLS) * SUB, 128), F32)

    def norm_window(i, _):
        base = pl.multiple_of(i * SLAB, SLAB)
        there, here = whole(i, srcs)
        pltpu.make_async_copy(there, here, sem_tok.at[i]).wait()
        tok[pl.ds(base + CELLS * SUB, (CELL_PAD - CELLS) * SUB), :] = pad_rows
        parts = [
            jnp.concatenate(
                [tok[pl.ds(base + g * 2 + lev, CELL_PAD, stride=SUB), :] for lev in range(2)], axis=0)
            for g in range(4)
        ]
        center = jnp.sum(parts[0] + parts[1] + parts[2] + parts[3], axis=1, keepdims=True) * (1.0 / D)
        parts = [p - center for p in parts]
        sq = [p * p for p in parts]
        spread = jnp.sum(sq[0] + sq[1] + sq[2] + sq[3], axis=1, keepdims=True) * (1.0 / D)
        scale = lax.rsqrt(spread + 1e-05)
        r = pl.ds(pl.multiple_of(i * TOK_PAD, TOK_PAD), TOK_PAD)
        for g in range(4):
            cols = slice(g * 128, (g + 1) * 128)
            y = parts[g] * scale * gain[:, cols] + shift[:, cols]
            hi, lo = hi_lo(y)
            xcat[r, g * 128:(g + 1) * 128] = hi
            xcat[r, D + g * 128:D + (g + 1) * 128] = lo
        return 0

    lax.fori_loop(0, nw, norm_window, 0)

    def split_q(t):
        cols = slice(t * D, (t + 1) * D)
        x = stage_q[:, cols]
        if t == 0:
            x = x * QSCALE
        hi, lo = hi_lo(x)
        wq[:D, cols] = hi
        wq[D:, cols] = lo

    def project(t):
        cols = slice(t * D, (t + 1) * D)
        qkv[:, cols] = (dot(xcat[:, :D], wq[:D, cols]) + dot(xcat[:, D:], wq[:D, cols])
                        + dot(xcat[:, :D], wq[D:, cols]))

    pad16 = jnp.zeros((128 - TOK_PAD, 128), F32)

    def turn(t, out):
        for i in range(nw):
            for g in range(4):
                x = qkv[i * TOK_PAD:(i + 1) * TOK_PAD, t * D + g * 128:t * D + (g + 1) * 128]
                hi, lo = hi_lo(jnp.concatenate([x, pad16], axis=0).T)
                top = i * 2 * D + g * 128
                out[top:top + 128, :] = hi
                out[top + D:top + D + 128, :] = lo

    copies_q[2].wait()
    if first:
        split_q(2)
    copies_q[0].wait()
    if first:
        split_q(0)
    project(2)
    for c in copies_b:
        c.wait()
    copies_q[1].wait()
    if first:
        split_q(1)
        copy_o.wait()
        hi, lo = hi_lo(stage_o[...])
        wo[:D, :] = hi
        wo[D:, :] = lo
    project(0)
    turn(2, v_t)
    project(1)
    turn(0, q_t)

    lat_at = lax.axis_index("lat")
    k_at = lax.broadcasted_iota(jnp.int32, (TOK_PAD, 128), 0)
    q_at = lax.broadcasted_iota(jnp.int32, (TOK_PAD, 128), 1)
    q_cell = jnp.where(q_at >= CELL_PAD, q_at - CELL_PAD, q_at)
    k_cell = jnp.where(k_at >= CELL_PAD, k_at - CELL_PAD, k_at)
    lane = lax.broadcasted_iota(jnp.int32, (TOK_PAD, 128), 1)
    for j, (b, _) in enumerate(runs):
        bias_v[j, 1600:, :] = jnp.zeros((bias_v.shape[1] - 1600, 100), F32)
        idq = jnp.zeros((TOK_PAD, 128), jnp.int32)
        idk = jnp.zeros((TOK_PAD, 128), jnp.int32)
        for i in range(WLAT):
            at = lat_at * ROWS + b * WLAT + i + HALF_LAT
            one = ids_ref[jnp.where(at >= 240, at - 240, at)]
            idq = jnp.where(q_cell >= i * WLON, one, idq)
            idk = jnp.where(k_cell >= i * WLON, one, idk)
        ok = jnp.logical_and(idq == idk, k_cell < CELLS)
        for h in range(HEADS):
            raw = jnp.concatenate(
                [bias_v[j, pl.ds(h, CELL_PAD, stride=HEADS), :],
                 bias_v[j, pl.ds(h + CELLS * HEADS, CELL_PAD, stride=HEADS), :],
                 jnp.zeros((128 - TOK_PAD, 100), F32)], axis=0) * LOG2E
            raw = jnp.concatenate([raw, jnp.zeros((128, 28), F32)], axis=1)
            moved = pltpu.roll(raw, CELL_PAD - CELLS, 1)
            wide = lax.broadcasted_iota(jnp.int32, (128, 128), 1)
            full = jnp.where(wide < CELL_PAD, raw, moved).T
            biasm[j, h] = jnp.where(ok, full[:TOK_PAD], NEG)

    if first:
        keep_q = pltpu.make_async_copy(wq, wq_out, sem_w.at[0])
        keep_q.start()
        keep_o = pltpu.make_async_copy(wo, wo_out, sem_w.at[1])
        keep_o.start()

    low_half = lane < 64
    blank = jnp.zeros((32, 128), BF)
    ends = []
    total = 0
    for _, ws in runs:
        total += len(ws)
        ends.append(total)

    def attend_window(i, _):
        r = pl.ds(pl.multiple_of(i * TOK_PAD, TOK_PAD), TOK_PAD)
        base = pl.multiple_of(i * 2 * D, 2 * D)
        slot = 0
        for e in ends[:-1]:
            slot = slot + jnp.where(i >= e, 1, 0)
        for g in range(4):
            k = qkv[r, D + g * 128:D + (g + 1) * 128]
            kh, kl = hi_lo(k)
            rkh = pltpu.roll(kh, 64, 1)
            rkl = pltpu.roll(kl, 64, 1)
            lhs_pairs = (
                jnp.concatenate([jnp.where(low_half, kh, rkl), kh[:, :64]], axis=1),
                jnp.concatenate([jnp.where(low_half, rkh, kl), rkh[:, :64]], axis=1),
            )
            outs = []
            for s in range(2):
                rows = []
                for part in (0, 0, D):
                    at = part + g * 128 + 64 * s
                    rows.append(jnp.concatenate([q_t[pl.ds(base + at, 32), :], blank], axis=1))
                    rows.append(jnp.concatenate([blank, q_t[pl.ds(base + at + 32, 32), :]], axis=1))
                scores = dot(lhs_pairs[s], jnp.concatenate(rows, axis=0))
                for t in range(2):
                    h = 2 * s + t
                    x = scores[:, t * 128:(t + 1) * 128] + biasm[slot, g * 4 + h]
                    x = jnp.exp2(x - jnp.max(x, axis=0, keepdims=True))
                    inv = 1.0 / jnp.sum(x, axis=0, keepdims=True)
                    hi, lo = hi_lo(x)
                    at = base + g * 128 + 32 * h
                    vals = jnp.concatenate([v_t[pl.ds(at, 32), :], v_t[pl.ds(at + D, 32), :]], axis=0)
                    both = dot(vals[:, :TOK_PAD], jnp.concatenate([hi, lo], axis=1))
                    both = both[:, :128] + both[:, 128:]
                    outs.append((both[:32] + both[32:]) * inv)
            hi, lo = hi_lo(jnp.concatenate(outs, axis=0).T[:TOK_PAD])
            hcat[r, g * 128:(g + 1) * 128] = hi
            hcat[r, D + g * 128:D + (g + 1) * 128] = lo
        return 0

    lax.fori_loop(0, nw, attend_window, 0, unroll=3)

    if not first:
        copy_o.wait()
    for t in range(2):
        cols = slice(t * 256, (t + 1) * 256)
        proj = (dot(hcat[:, :D], wo[:D, cols]) + dot(hcat[:, D:], wo[:D, cols])
                + dot(hcat[:, :D], wo[D:, cols]))
        for i in range(nw):
            for lev in range(2):
                top = i * TOK_PAD + lev * CELL_PAD
                for g in range(2):
                    at = pl.ds(i * SLAB + (2 * t + g) * 2 + lev, CELL_PAD, stride=SUB)
                    tok[at, :] = tok[at, :] + proj[top:top + CELL_PAD, g * 128:(g + 1) * 128]
    for i in range(nw):
        move(i, dsts, False, sem_out.at[i])
    if first:
        keep_q.wait()
        keep_o.wait()
    for i in range(nw):
        there, here = whole(i, dsts)
        pltpu.make_async_copy(here, there, sem_out.at[i]).wait()


def group_call(runs, ids, tok, halos, gain, shift, w_qkv, w_out, bias, out_so_far, name):
    nw = sum(len(ws) for _, ws in runs)
    nb = len(runs)
    halo = halos is not None
    aliased = out_so_far is not None
    first = w_qkv.dtype == F32
    any_spec = pl.BlockSpec(memory_space=pl.ANY)
    hbm_spec = pl.BlockSpec(memory_space=pltpu.HBM)
    vmem_spec = pl.BlockSpec(memory_space=pltpu.VMEM)
    smem_spec = pl.BlockSpec(memory_space=pltpu.SMEM)
    args = [ids, tok]
    specs = [smem_spec, hbm_spec]
    if halo:
        args += list(halos)
        specs += [any_spec] * 3
    args += [gain, shift, w_qkv, w_out, bias]
    specs += [vmem_spec, vmem_spec, hbm_spec, hbm_spec, hbm_spec]
    aliases = {}
    if aliased:
        aliases = {len(args): 0}
        args.append(out_so_far)
        specs.append(hbm_spec)
    out_shapes = [jax.ShapeDtypeStruct(tok.shape, F32)]
    if halo:
        out_shapes += [jax.ShapeDtypeStruct(h.shape, F32) for h in halos]
    if first:
        out_shapes += [jax.ShapeDtypeStruct((2 * D, 3 * D), BF), jax.ShapeDtypeStruct((2 * D, D), BF)]
    stages = [pltpu.VMEM((D, 3 * D), F32), pltpu.VMEM((D, D), F32)] if first else []
    rows_all = nw * TOK_PAD
    return pl.pallas_call(
        functools.partial(group_kernel, runs, halo, aliased, first),
        out_shape=out_shapes,
        in_specs=specs,
        out_specs=[hbm_spec] * len(out_shapes),
        input_output_aliases=aliases,
        scratch_shapes=[
            pltpu.VMEM((nw * WIN_ROWS, WLON * SUB, 128), F32),
            pltpu.VMEM((nb, 1712, 100), F32),
            pltpu.VMEM((2 * D, 3 * D), BF),
            pltpu.VMEM((2 * D, D), BF),
            pltpu.VMEM((rows_all, 2 * D), BF),
            pltpu.VMEM((rows_all, 3 * D), F32),
            pltpu.VMEM((nw * 2 * D, 128), BF),
            pltpu.VMEM((nw * 2 * D, 128), BF),
            pltpu.VMEM((rows_all, 2 * D), BF),
            pltpu.VMEM((nb, HEADS, TOK_PAD, 128), F32),
            pltpu.SemaphoreType.DMA((nw,)),
            pltpu.SemaphoreType.DMA((TILES + 1,)),
            pltpu.SemaphoreType.DMA((nb,)),
            pltpu.SemaphoreType.DMA((nw,)),
        ] + stages,
        compiler_params=pltpu.CompilerParams(vmem_limit_bytes=(52 if halo else 56) << 20),
        cost_estimate=pl.CostEstimate(
            flops=nw * 10**9, bytes_accessed=8 << 20, transcendentals=nw * 200000),
        name=name,
    )(*args)


def rim_parts(whole_ref, s_ref, e_ref, c_ref):
    edge = HALF_LON * SUB
    return (
        (s_ref, whole_ref.at[pl.ds(0, HALF_LAT), pl.ds(edge, S_COLS * SUB)]),
        (e_ref, whole_ref.at[pl.ds(HALF_LAT, ROWS - HALF_LAT), pl.ds(0, edge)]),
        (c_ref, whole_ref.at[pl.ds(0, HALF_LAT), pl.ds(0, edge)]),
    )


def merge_kernel(s_ref, e_ref, c_ref, _, out_ref, sem):
    copies = [pltpu.make_async_copy(part, place, sem.at[n])
              for n, (part, place) in enumerate(rim_parts(out_ref, s_ref, e_ref, c_ref))]
    for c in copies:
        c.start()
    for c in copies:
        c.wait()


def pack_kernel(tok_ref, s_ref, e_ref, c_ref, sem):
    copies = [pltpu.make_async_copy(place, part, sem.at[n])
              for n, (part, place) in enumerate(rim_parts(tok_ref, s_ref, e_ref, c_ref))]
    for c in copies:
        c.start()
    for c in copies:
        c.wait()


def pack_call(tok):
    edge = HALF_LON * SUB
    return pl.pallas_call(
        pack_kernel,
        out_shape=[jax.ShapeDtypeStruct((HALF_LAT, S_COLS * SUB, 128), F32),
                   jax.ShapeDtypeStruct((ROWS - HALF_LAT, edge, 128), F32),
                   jax.ShapeDtypeStruct((HALF_LAT, edge, 128), F32)],
        in_specs=[pl.BlockSpec(memory_space=pltpu.HBM)],
        out_specs=[pl.BlockSpec(memory_space=pl.ANY)] * 3,
        scratch_shapes=[pltpu.SemaphoreType.DMA((3,))],
        compiler_params=pltpu.CompilerParams(vmem_limit_bytes=52 << 20),
        name="pack",
    )(tok)


def merge_call(s, e, c, out_so_far):
    any_spec = pl.BlockSpec(memory_space=pl.ANY)
    return pl.pallas_call(
        merge_kernel,
        out_shape=jax.ShapeDtypeStruct(out_so_far.shape, F32),
        in_specs=[any_spec] * 3 + [pl.BlockSpec(memory_space=pltpu.HBM)],
        out_specs=pl.BlockSpec(memory_space=pltpu.HBM),
        input_output_aliases={3: 0},
        scratch_shapes=[pltpu.SemaphoreType.DMA((3,))],
        compiler_params=pltpu.CompilerParams(vmem_limit_bytes=4 << 20),
        name="merge",
    )(s, e, c, out_so_far)


def shift_pairs(dlon, dlat):
    n_lon, n_lat = lax.axis_size("lon"), lax.axis_size("lat")
    pairs = []
    for lon in range(n_lon):
        for lat in range(n_lat):
            to = ((lon + dlon) % n_lon) * n_lat + (lat + dlat) % n_lat
            pairs.append((lon * n_lat + lat, to))
    return pairs


def send(value, dlon, dlat):
    return lax.ppermute(value, ("lon", "lat"), shift_pairs(dlon, dlat))


def body(tokens, ln_gain, ln_shift, w_qkv, w_out, region_ids, position_bias):
    tok = tokens.transpose(1, 2, 0, 3).reshape(ROWS, COLS, 2, 4, 128)
    tok = tok.transpose(0, 1, 3, 2, 4).reshape(ROWS, COLS * SUB, 128)
    bias = position_bias.transpose(0, 2, 1, 3).reshape(BANDS * 100 * HEADS, 100)
    s, e, c = pack_call(tok)
    s = send(s, 0, -1)
    e = send(e, -1, 0)
    c = send(c, -1, -1)
    common = (ln_gain, ln_shift, w_qkv, w_out, bias)
    inner = tuple(range(ACROSS - 1))
    out, wq, wo = group_call(((0, inner),), region_ids, tok, None, *common, None, "band0")
    common = (ln_gain, ln_shift, wq, wo, bias)
    out, s, e, c = group_call(
        ((2, tuple(range(ACROSS))), (0, (ACROSS - 1,)), (1, (ACROSS - 1,))),
        region_ids, tok, (s, e, c), *common, out, "rim")
    s = send(s, 0, 1)
    e = send(e, 1, 0)
    c = send(c, 1, 1)
    (out,) = group_call(((1, inner),), region_ids, tok, None, *common, out, "band1")
    out = merge_call(s, e, c, out)
    out = out.reshape(ROWS, COLS, 4, 2, 128).transpose(0, 1, 3, 2, 4).reshape(ROWS, COLS, 2, D)
    return out.transpose(2, 0, 1, 3)


def solution(mesh):
    in_specs = (P(None, "lat", "lon", None), P(), P(), P(), P(), P(), P("lat", None, None, None))
    out_specs = P(None, "lat", "lon", None)
    return jax.shard_map(body, mesh=mesh, in_specs=in_specs, out_specs=out_specs, check_vma=False)
```

time: 104 us -> 81.8 us (0.79)
  Pallas kernels: 84.9 us -> 68.5 us
  local copies, waits for them, and re-layouts: 6.13 us -> 0.9 us
    pallas_call x3 -> x4, Pallas kernels: 82.6 us -> 67.5 us  [the longest x3 66.3 us: group_call(): pl.pallas_call(functools.partial(group_kernel, runs, halo, aliased, first...]
    slice x3 -> x0, local copies, waits for them, and re-layouts: 2.93 us -> none  [the longest x1 1.18 us: body(): s = send(tok[:HALF_LAT, edge:].reshape(-1, 128), 0, -1)]
    unnamed x12 -> x8, local copies, waits for them, and re-layouts: 3.19 us -> 0.9 us
    pallas_call x1, Pallas kernels: 2.32 us -> 0.99 us  [merge_call(): pl.pallas_call(merge_kernel, out_shape=jax.ShapeDtypeStruct(out_so_far.sh...]
  transfers between devices with their start and end apart: 6 -> 6, of which waited for: 0 -> 0; matrix products, arithmetic and copies ran while one was open for 2% -> 0% of each run, Pallas kernels for 48% -> 50%
where the time goes in v1:
time: 81.8 us; the launch traced here: 81.6 us
  Pallas kernels  68.5 us (84%)
  starting transfers between devices  11.9 us (15%)
  local copies, waits for them, and re-layouts  0.9 us (1%)
    pallas_call x3, Pallas kernels, group_call(): pl.pallas_call(functools.partial(group_kernel, runs, halo, aliased, first...  66.3 us
    ppermute x6, starting transfers between devices, send(): return lax.ppermute(value, ('lon', 'lat'), shift_pairs(dlon, dlat))  11.9 us
  transfers between devices with their start and end apart: 6, of which 0 were waited for; matrix products, arithmetic and copies ran while one was open for 0% of the time, Pallas kernels for 50%

profile of v1, /device:TPU:0, one launch (start us, length us, event | category | flops | bytes accessed | tf_op | source)
XLA Modules:
  0.0 81.6 jit_solution(13754820176771899360)
XLA Ops:
  0.0 1.2 %pack.1 = (f32[2,760,128]{2,1,0:T(8,128)S(1)}, f32[13,40,128]{2,1,0:T(8,128)S(1)}, f32[2,40,128]{2,1,0:T(8,128)S(1)}) custom-call(f32[15,800,128]{2,1,0:T(8,128)} %bitcast.17), custom_call_target="tpu_custom_call" | custom-call | tf_op jit(solution)/shard_map/pack/pallas_call | solution.py:388
  1.2 8.3 %collective-permute-start.2 = (f32[2,40,128]{2,1,0:T(8,128)S(1)}, f32[2,40,128]{2,1,0:T(8,128)S(1)}, u32[]{:S(2)}, u32[]{:S(2)}) collective-permute-start(f32[2,40,128]{2,1,0:T(8,128)S(1)} %get-tuple-element.17), channel_id=1, source_target_pairs={{0,127},{1,112},{2,113},{3,114},{4,115},{5,116},{6,117},{7,118},{8... | collective-permute-start | bytes 122888 | tf_op jit(solution)/shard_map/ppermute | solution.py:426
  9.5 1.1 %collective-permute-start.1 = (f32[13,40,128]{2,1,0:T(8,128)S(1)}, f32[13,40,128]{2,1,0:T(8,128)S(1)}, u32[]{:S(2)}, u32[]{:S(2)}) collective-permute-start(f32[13,40,128]{2,1,0:T(8,128)S(1)} %get-tuple-element.16), channel_id=1, source_target_pairs={{0,112},{1,113},{2,114},{3,115},{4,116},{5,117},{6,118},{7,119},{8... | collective-permute-start | bytes 798728 | tf_op jit(solution)/shard_map/ppermute | solution.py:426
  10.6 1.2 %collective-permute-start = (f32[2,760,128]{2,1,0:T(8,128)S(1)}, f32[2,760,128]{2,1,0:T(8,128)S(1)}, u32[]{:S(2)}, u32[]{:S(2)}) collective-permute-start(f32[2,760,128]{2,1,0:T(8,128)S(1)} %get-tuple-element.15), channel_id=1, source_target_pairs={{0,15},{1,0},{2,1},{3,2},{4,3},{5,4},{6,5},{7,6},{8,7},{9,8},{10,9... | collective-permute-start | bytes 2334728 | tf_op jit(solution)/shard_map/ppermute | solution.py:426
  11.8 0.0 copy-start
  11.8 0.0 copy-start.1
  11.8 20.6 %band0.1 = (f32[15,800,128]{2,1,0:T(8,128)}, bf16[1024,1536]{1,0:T(8,128)(2,1)}, bf16[1024,512]{1,0:T(8,128)(2,1)}) custom-call(s32[240]{0:T(256)} %refs_0_.5, f32[15,800,128]{2,1,0:T(8,128)} %bitcast.18, f32[512]{0:T(512)} %refs_2_.3, f32[512]{0:T(512)} %refs_3_.3, f32[512,1536]{1,0:T(8,128)} %refs_4_.1, f32[512,512]{1,0:T(8,128)} %refs_5_.2, ...), custom_call_target="tpu_custom_call" | custom-call | flops 8999999488 | bytes 8388608 | tf_op jit(solution)/shard_map/band0/pallas_call | solution.py:330
  32.4 0.0 collective-permute-done.2.refs_4_
  32.5 0.0 collective-permute-done.1.refs_3_
  32.5 0.0 collective-permute-done.refs_2_
  32.5 0.0 copy-start.3
  32.5 0.9 %copy-done.3 = f32[2,760,128]{2,1,0:T(8,128)} copy-done((f32[2,760,128]{2,1,0:T(8,128)}, f32[2,760,128]{2,1,0:T(8,128)S(1)}, u32[]{:S(2)}) %copy-start.3) | copy-done | bytes 778264
  33.4 0.0 copy-done
  33.4 0.0 copy-done.1
  33.4 0.0 copy-done.2
  33.4 25.9 %rim.1 = (f32[15,800,128]{2,1,0:T(8,128)}, f32[2,760,128]{2,1,0:T(8,128)S(1)}, f32[13,40,128]{2,1,0:T(8,128)S(1)}, f32[2,40,128]{2,1,0:T(8,128)S(1)}) custom-call(s32[240]{0:T(256)S(1)} %copy-done.2, f32[15,800,128]{2,1,0:T(8,128)} %bitcast.19, f32[2,760,128]{2,1,0:T(8,128)} %copy-done.3, ...), custom_call_target="tpu_custom_call", output_to_operand_aliasing={{0}: (10, {})} | custom-call | flops 12000000000 | bytes 8388608 | tf_op jit(solution)/shard_map/rim/pallas_call | solution.py:330
  59.3 0.1 collective-permute-start.5
  59.4 1.3 %collective-permute-start.4 = (f32[13,40,128]{2,1,0:T(8,128)S(1)}, f32[13,40,128]{2,1,0:T(8,128)S(1)}, u32[]{:S(2)}, u32[]{:S(2)}) collective-permute-start(f32[13,40,128]{2,1,0:T(8,128)S(1)} %get-tuple-element.22), channel_id=1, source_target_pairs={{0,16},{1,17},{2,18},{3,19},{4,20},{5,21},{6,22},{7,23},{8,24},{9,... | collective-permute-start | bytes 798728 | tf_op jit(solution)/shard_map/ppermute | solution.py:426
  60.6 0.0 collective-permute-start.3
  60.6 19.8 %band1.1._ = f32[15,800,128]{2,1,0:T(8,128)} custom-call(s32[240]{0:T(256)} %refs_0_.5, f32[15,800,128]{2,1,0:T(8,128)} %bitcast.20, f32[512]{0:T(512)} %refs_2_.3, f32[512]{0:T(512)} %refs_3_.3, bf16[1024,1536]{1,0:T(8,128)(2,1)} %get-tuple-element.18.refs_7_.refs_4_, ...), custom_call_target="tpu_custom_call", output_to_operand_aliasing={{}: (7, {})} | custom-call | flops 8999999488 | bytes 8388608 | tf_op jit(solution)/shard_map/band1/pallas_call | solution.py:330
  80.4 0.0 collective-permute-done.5.c_ref
  80.4 0.0 collective-permute-done.4.e_ref
  80.5 0.0 collective-permute-done.3.s_ref
  80.5 1.0 %merge.1 = f32[15,800,128]{2,1,0:T(8,128)} custom-call(f32[2,760,128]{2,1,0:T(8,128)S(1)} %collective-permute-done.3.s_ref, f32[13,40,128]{2,1,0:T(8,128)S(1)} %collective-permute-done.4.e_ref, f32[2,40,128]{2,1,0:T(8,128)S(1)} %collective-permute-done.5.c_ref, f32[15,800,128]{2,1,0:T(8,128)} %band1.1._), custom_call_target="tpu_custom_call", output_to_operand_aliasing={{}: (3, {})} | custom-call | tf_op jit(solution)/shard_map/merge/pallas_call | solution.py:403
  (1 shorter events, 0.0 us)
Async XLA Ops:
  1.2 31.2 %collective-permute-start.2 = (f32[2,40,128]{2,1,0:T(8,128)S(1)}, f32[2,40,128]{2,1,0:T(8,128)S(1)}, u32[]{:S(2)}, u32[]{:S(2)}) collective-permute-start(f32[2,40,128]{2,1,0:T(8,128)S(1)} %get-tuple-element.17), channel_id=1, source_target_pairs={{0,127},{1,112},{2,113},{3,114},{4,115},{5,116},{6,117},{7,118},{8... | collective-permute-start | bytes 122888 | tf_op jit(solution)/shard_map/ppermute | solution.py:426
  9.5 23.0 %collective-permute-start.1 = (f32[13,40,128]{2,1,0:T(8,128)S(1)}, f32[13,40,128]{2,1,0:T(8,128)S(1)}, u32[]{:S(2)}, u32[]{:S(2)}) collective-permute-start(f32[13,40,128]{2,1,0:T(8,128)S(1)} %get-tuple-element.16), channel_id=1, source_target_pairs={{0,112},{1,113},{2,114},{3,115},{4,116},{5,117},{6,118},{7,119},{8... | collective-permute-start | bytes 798728 | tf_op jit(solution)/shard_map/ppermute | solution.py:426
  10.6 21.8 %collective-permute-start = (f32[2,760,128]{2,1,0:T(8,128)S(1)}, f32[2,760,128]{2,1,0:T(8,128)S(1)}, u32[]{:S(2)}, u32[]{:S(2)}) collective-permute-start(f32[2,760,128]{2,1,0:T(8,128)S(1)} %get-tuple-element.15), channel_id=1, source_target_pairs={{0,15},{1,0},{2,1},{3,2},{4,3},{5,4},{6,5},{7,6},{8,7},{9,8},{10,9... | collective-permute-start | bytes 2334728 | tf_op jit(solution)/shard_map/ppermute | solution.py:426
  11.8 21.6 %copy-start = (f32[512]{0:T(512)S(1)}, f32[512]{0:T(512)}, u32[]{:S(2)}) copy-start(f32[512]{0:T(512)} %refs_2_.3) | copy-start | bytes 6148
  11.8 21.6 %copy-start.1 = (f32[512]{0:T(512)S(1)}, f32[512]{0:T(512)}, u32[]{:S(2)}) copy-start(f32[512]{0:T(512)} %refs_3_.3) | copy-start | bytes 6148
  11.8 21.6 %copy-start.2 = (s32[240]{0:T(256)S(1)}, s32[240]{0:T(256)}, u32[]{:S(2)}) copy-start(s32[240]{0:T(256)} %refs_0_.5) | copy-start | bytes 2884
  32.5 0.9 %copy-start.3 = (f32[2,760,128]{2,1,0:T(8,128)}, f32[2,760,128]{2,1,0:T(8,128)S(1)}, u32[]{:S(2)}) copy-start(f32[2,760,128]{2,1,0:T(8,128)S(1)} %collective-permute-done.refs_2_) | copy-start | bytes 2334724
  59.3 21.1 %collective-permute-start.5 = (f32[2,40,128]{2,1,0:T(8,128)S(1)}, f32[2,40,128]{2,1,0:T(8,128)S(1)}, u32[]{:S(2)}, u32[]{:S(2)}) collective-permute-start(f32[2,40,128]{2,1,0:T(8,128)S(1)} %get-tuple-element.23), channel_id=1, source_target_pairs={{0,17},{1,18},{2,19},{3,20},{4,21},{5,22},{6,23},{7,24},{8,25},{9,... | collective-permute-start | bytes 122888 | tf_op jit(solution)/shard_map/ppermute | solution.py:426
  59.4 21.1 %collective-permute-start.4 = (f32[13,40,128]{2,1,0:T(8,128)S(1)}, f32[13,40,128]{2,1,0:T(8,128)S(1)}, u32[]{:S(2)}, u32[]{:S(2)}) collective-permute-start(f32[13,40,128]{2,1,0:T(8,128)S(1)} %get-tuple-element.22), channel_id=1, source_target_pairs={{0,16},{1,17},{2,18},{3,19},{4,20},{5,21},{6,22},{7,23},{8,24},{9,... | collective-permute-start | bytes 798728 | tf_op jit(solution)/shard_map/ppermute | solution.py:426
  60.6 19.8 %collective-permute-start.3 = (f32[2,760,128]{2,1,0:T(8,128)S(1)}, f32[2,760,128]{2,1,0:T(8,128)S(1)}, u32[]{:S(2)}, u32[]{:S(2)}) collective-permute-start(f32[2,760,128]{2,1,0:T(8,128)S(1)} %get-tuple-element.21), channel_id=1, source_target_pairs={{0,1},{1,2},{2,3},{3,4},{4,5},{5,6},{6,7},{7,8},{8,9},{9,10},{10,1... | collective-permute-start | bytes 2334728 | tf_op jit(solution)/shard_map/ppermute | solution.py:426

commit v2 on v1

--- a/solution.py
+++ b/solution.py
@@ -28,6 +28,8 @@
 NEG = -1e30
 LOG2E = math.log2(math.e)
 TILES = 3
+UNROLL = 3
+AHEAD = 6
 QSCALE = LOG2E / math.sqrt(D // HEADS)
 BF = jnp.bfloat16
 F32 = jnp.float32
@@ -235,46 +237,62 @@
         total += len(ws)
         ends.append(total)
 
-    def attend_window(i, _):
-        r = pl.ds(pl.multiple_of(i * TOK_PAD, TOK_PAD), TOK_PAD)
-        base = pl.multiple_of(i * 2 * D, 2 * D)
-        slot = 0
-        for e in ends[:-1]:
-            slot = slot + jnp.where(i >= e, 1, 0)
-        for g in range(4):
-            k = qkv[r, D + g * 128:D + (g + 1) * 128]
-            kh, kl = hi_lo(k)
-            rkh = pltpu.roll(kh, 64, 1)
-            rkl = pltpu.roll(kl, 64, 1)
-            lhs_pairs = (
-                jnp.concatenate([jnp.where(low_half, kh, rkl), kh[:, :64]], axis=1),
-                jnp.concatenate([jnp.where(low_half, rkh, kl), rkh[:, :64]], axis=1),
-            )
-            outs = []
-            for s in range(2):
-                rows = []
-                for part in (0, 0, D):
-                    at = part + g * 128 + 64 * s
-                    rows.append(jnp.concatenate([q_t[pl.ds(base + at, 32), :], blank], axis=1))
-                    rows.append(jnp.concatenate([blank, q_t[pl.ds(base + at + 32, 32), :]], axis=1))
-                scores = dot(lhs_pairs[s], jnp.concatenate(rows, axis=0))
-                for t in range(2):
-                    h = 2 * s + t
-                    x = scores[:, t * 128:(t + 1) * 128] + biasm[slot, g * 4 + h]
-                    x = jnp.exp2(x - jnp.max(x, axis=0, keepdims=True))
-                    inv = 1.0 / jnp.sum(x, axis=0, keepdims=True)
-                    hi, lo = hi_lo(x)
-                    at = base + g * 128 + 32 * h
-                    vals = jnp.concatenate([v_t[pl.ds(at, 32), :], v_t[pl.ds(at + D, 32), :]], axis=0)
-                    both = dot(vals[:, :TOK_PAD], jnp.concatenate([hi, lo], axis=1))
-                    both = both[:, :128] + both[:, 128:]
-                    outs.append((both[:32] + both[32:]) * inv)
-            hi, lo = hi_lo(jnp.concatenate(outs, axis=0).T[:TOK_PAD])
-            hcat[r, g * 128:(g + 1) * 128] = hi
-            hcat[r, D + g * 128:D + (g + 1) * 128] = lo
+    def attend_windows(step, _):
+        items = [(u, g, s) for u in range(UNROLL) for g in range(4) for s in range(2)]
+        keys, raw, outs = {}, {}, {}
+        at_window = []
+        for u in range(UNROLL):
+            i = step * UNROLL + u
+            slot = 0
+            for e in ends[:-1]:
+                slot = slot + jnp.where(i >= e, 1, 0)
+            at_window.append((pl.ds(pl.multiple_of(i * TOK_PAD, TOK_PAD), TOK_PAD),
+                              pl.multiple_of(i * 2 * D, 2 * D), slot))
+
+        def score(u, g, s):
+            r, base, _ = at_window[u]
+            if s == 0:
+                kh, kl = hi_lo(qkv[r, D + g * 128:D + (g + 1) * 128])
+                rkh = pltpu.roll(kh, 64, 1)
+                rkl = pltpu.roll(kl, 64, 1)
+                keys[u, g] = (
+                    jnp.concatenate([jnp.where(low_half, kh, rkl), kh[:, :64]], axis=1),
+                    jnp.concatenate([jnp.where(low_half, rkh, kl), rkh[:, :64]], axis=1),
+                )
+            rows = []
+            for part in (0, 0, D):
+                at = base + part + g * 128 + 64 * s
+                rows.append(jnp.concatenate([q_t[pl.ds(at, 32), :], blank], axis=1))
+                rows.append(jnp.concatenate([blank, q_t[pl.ds(at + 32, 32), :]], axis=1))
+            raw[u, g, s] = dot(keys[u, g][s], jnp.concatenate(rows, axis=0))
+
+        def mix(u, g, s):
+            r, base, slot = at_window[u]
+            scores = raw.pop((u, g, s))
+            for t in range(2):
+                h = 2 * s + t
+                x = scores[:, t * 128:(t + 1) * 128] + biasm[slot, g * 4 + h]
+                x = jnp.exp2(x - jnp.max(x, axis=0, keepdims=True))
+                inv = 1.0 / jnp.sum(x, axis=0, keepdims=True)
+                hi, lo = hi_lo(x)
+                at = base + g * 128 + 32 * h
+                vals = jnp.concatenate([v_t[pl.ds(at, 32), :], v_t[pl.ds(at + D, 32), :]], axis=0)
+                both = dot(vals[:, :TOK_PAD], jnp.concatenate([hi, lo], axis=1))
+                both = both[:, :128] + both[:, 128:]
+                outs.setdefault((u, g), []).append((both[:32] + both[32:]) * inv)
+            if s == 1:
+                hi, lo = hi_lo(jnp.concatenate(outs.pop((u, g)), axis=0).T[:TOK_PAD])
+                hcat[r, g * 128:(g + 1) * 128] = hi
+                hcat[r, D + g * 128:D + (g + 1) * 128] = lo
+
+        for n in range(len(items) + AHEAD):
+            if n < len(items):
+                score(*items[n])
+            if n >= AHEAD:
+                mix(*items[n - AHEAD])
         return 0
 
-    lax.fori_loop(0, nw, attend_window, 0, unroll=3)
+    lax.fori_loop(0, nw // UNROLL, attend_windows, 0)
 
     if not first:
         copy_o.wait()

time: 81.8 us -> 74.3 us (0.908)
  Pallas kernels: 68.5 us -> 61 us
    pallas_call x3, Pallas kernels: 66.3 us -> 58.8 us  [group_call(): pl.pallas_call(functools.partial(group_kernel, runs, halo, aliased, first...]
  transfers between devices with their start and end apart: 6 -> 6, of which waited for: 0 -> 0; matrix products, arithmetic and copies ran while one was open for 0% -> 0% of each run, Pallas kernels for 50% -> 48%
where the time goes in v2:
time: 74.3 us; the launch traced here: 74.1 us
  Pallas kernels  61 us (82%)
  starting transfers between devices  11.9 us (16%)
  local copies, waits for them, and re-layouts  0.9 us (1%)
    pallas_call x3, Pallas kernels, group_call(): pl.pallas_call(functools.partial(group_kernel, runs, halo, aliased, first...  58.8 us
    ppermute x6, starting transfers between devices, send(): return lax.ppermute(value, ('lon', 'lat'), shift_pairs(dlon, dlat))  11.9 us
  transfers between devices with their start and end apart: 6, of which 0 were waited for; matrix products, arithmetic and copies ran while one was open for 0% of the time, Pallas kernels for 48%

profile of v2, /device:TPU:0, one launch (start us, length us, event | category | flops | bytes accessed | tf_op | source)
XLA Modules:
  0.0 74.1 jit_solution(14359223085661108280)
XLA Ops:
  0.0 1.2 %pack.1 = (f32[2,760,128]{2,1,0:T(8,128)S(1)}, f32[13,40,128]{2,1,0:T(8,128)S(1)}, f32[2,40,128]{2,1,0:T(8,128)S(1)}) custom-call(f32[15,800,128]{2,1,0:T(8,128)} %bitcast.17), custom_call_target="tpu_custom_call" | custom-call | tf_op jit(solution)/shard_map/pack/pallas_call | solution.py:406
  1.2 8.3 %collective-permute-start.2 = (f32[2,40,128]{2,1,0:T(8,128)S(1)}, f32[2,40,128]{2,1,0:T(8,128)S(1)}, u32[]{:S(2)}, u32[]{:S(2)}) collective-permute-start(f32[2,40,128]{2,1,0:T(8,128)S(1)} %get-tuple-element.17), channel_id=1, source_target_pairs={{0,127},{1,112},{2,113},{3,114},{4,115},{5,116},{6,117},{7,118},{8... | collective-permute-start | bytes 122888 | tf_op jit(solution)/shard_map/ppermute | solution.py:444
  9.5 1.1 %collective-permute-start.1 = (f32[13,40,128]{2,1,0:T(8,128)S(1)}, f32[13,40,128]{2,1,0:T(8,128)S(1)}, u32[]{:S(2)}, u32[]{:S(2)}) collective-permute-start(f32[13,40,128]{2,1,0:T(8,128)S(1)} %get-tuple-element.16), channel_id=1, source_target_pairs={{0,112},{1,113},{2,114},{3,115},{4,116},{5,117},{6,118},{7,119},{8... | collective-permute-start | bytes 798728 | tf_op jit(solution)/shard_map/ppermute | solution.py:444
  10.6 1.2 %collective-permute-start = (f32[2,760,128]{2,1,0:T(8,128)S(1)}, f32[2,760,128]{2,1,0:T(8,128)S(1)}, u32[]{:S(2)}, u32[]{:S(2)}) collective-permute-start(f32[2,760,128]{2,1,0:T(8,128)S(1)} %get-tuple-element.15), channel_id=1, source_target_pairs={{0,15},{1,0},{2,1},{3,2},{4,3},{5,4},{6,5},{7,6},{8,7},{9,8},{10,9... | collective-permute-start | bytes 2334728 | tf_op jit(solution)/shard_map/ppermute | solution.py:444
  11.8 0.0 copy-start
  11.8 0.0 copy-start.1
  11.8 18.3 %band0.1 = (f32[15,800,128]{2,1,0:T(8,128)}, bf16[1024,1536]{1,0:T(8,128)(2,1)}, bf16[1024,512]{1,0:T(8,128)(2,1)}) custom-call(s32[240]{0:T(256)} %refs_0_.5, f32[15,800,128]{2,1,0:T(8,128)} %bitcast.18, f32[512]{0:T(512)} %refs_2_.3, f32[512]{0:T(512)} %refs_3_.3, f32[512,1536]{1,0:T(8,128)} %refs_4_.1, f32[512,512]{1,0:T(8,128)} %refs_5_.2, ...), custom_call_target="tpu_custom_call" | custom-call | flops 8999999488 | bytes 8388608 | tf_op jit(solution)/shard_map/band0/pallas_call | solution.py:348
  30.1 0.0 collective-permute-done.2.refs_4_
  30.1 0.0 collective-permute-done.1.refs_3_
  30.1 0.0 collective-permute-done.refs_2_
  30.1 0.0 copy-start.3
  30.1 0.9 %copy-done.3 = f32[2,760,128]{2,1,0:T(8,128)} copy-done((f32[2,760,128]{2,1,0:T(8,128)}, f32[2,760,128]{2,1,0:T(8,128)S(1)}, u32[]{:S(2)}) %copy-start.3) | copy-done | bytes 778264
  31.0 0.0 copy-done
  31.0 0.0 copy-done.1
  31.0 0.0 copy-done.2
  31.0 23.1 %rim.1 = (f32[15,800,128]{2,1,0:T(8,128)}, f32[2,760,128]{2,1,0:T(8,128)S(1)}, f32[13,40,128]{2,1,0:T(8,128)S(1)}, f32[2,40,128]{2,1,0:T(8,128)S(1)}) custom-call(s32[240]{0:T(256)S(1)} %copy-done.2, f32[15,800,128]{2,1,0:T(8,128)} %bitcast.19, f32[2,760,128]{2,1,0:T(8,128)} %copy-done.3, ...), custom_call_target="tpu_custom_call", output_to_operand_aliasing={{0}: (10, {})} | custom-call | flops 12000000000 | bytes 8388608 | tf_op jit(solution)/shard_map/rim/pallas_call | solution.py:348
  54.1 0.1 collective-permute-start.5
  54.2 1.3 %collective-permute-start.4 = (f32[13,40,128]{2,1,0:T(8,128)S(1)}, f32[13,40,128]{2,1,0:T(8,128)S(1)}, u32[]{:S(2)}, u32[]{:S(2)}) collective-permute-start(f32[13,40,128]{2,1,0:T(8,128)S(1)} %get-tuple-element.22), channel_id=1, source_target_pairs={{0,16},{1,17},{2,18},{3,19},{4,20},{5,21},{6,22},{7,23},{8,24},{9,... | collective-permute-start | bytes 798728 | tf_op jit(solution)/shard_map/ppermute | solution.py:444
  55.5 0.0 collective-permute-start.3
  55.5 17.4 %band1.1._ = f32[15,800,128]{2,1,0:T(8,128)} custom-call(s32[240]{0:T(256)} %refs_0_.5, f32[15,800,128]{2,1,0:T(8,128)} %bitcast.20, f32[512]{0:T(512)} %refs_2_.3, f32[512]{0:T(512)} %refs_3_.3, bf16[1024,1536]{1,0:T(8,128)(2,1)} %get-tuple-element.18.refs_7_.refs_4_, ...), custom_call_target="tpu_custom_call", output_to_operand_aliasing={{}: (7, {})} | custom-call | flops 8999999488 | bytes 8388608 | tf_op jit(solution)/shard_map/band1/pallas_call | solution.py:348
  72.9 0.0 collective-permute-done.5.c_ref
  72.9 0.0 collective-permute-done.4.e_ref
  72.9 0.0 collective-permute-done.3.s_ref
  72.9 1.0 %merge.1 = f32[15,800,128]{2,1,0:T(8,128)} custom-call(f32[2,760,128]{2,1,0:T(8,128)S(1)} %collective-permute-done.3.s_ref, f32[13,40,128]{2,1,0:T(8,128)S(1)} %collective-permute-done.4.e_ref, f32[2,40,128]{2,1,0:T(8,128)S(1)} %collective-permute-done.5.c_ref, f32[15,800,128]{2,1,0:T(8,128)} %band1.1._), custom_call_target="tpu_custom_call", output_to_operand_aliasing={{}: (3, {})} | custom-call | tf_op jit(solution)/shard_map/merge/pallas_call | solution.py:421
  (1 shorter events, 0.0 us)
Async XLA Ops:
  1.2 28.9 %collective-permute-start.2 = (f32[2,40,128]{2,1,0:T(8,128)S(1)}, f32[2,40,128]{2,1,0:T(8,128)S(1)}, u32[]{:S(2)}, u32[]{:S(2)}) collective-permute-start(f32[2,40,128]{2,1,0:T(8,128)S(1)} %get-tuple-element.17), channel_id=1, source_target_pairs={{0,127},{1,112},{2,113},{3,114},{4,115},{5,116},{6,117},{7,118},{8... | collective-permute-start | bytes 122888 | tf_op jit(solution)/shard_map/ppermute | solution.py:444
  9.5 20.6 %collective-permute-start.1 = (f32[13,40,128]{2,1,0:T(8,128)S(1)}, f32[13,40,128]{2,1,0:T(8,128)S(1)}, u32[]{:S(2)}, u32[]{:S(2)}) collective-permute-start(f32[13,40,128]{2,1,0:T(8,128)S(1)} %get-tuple-element.16), channel_id=1, source_target_pairs={{0,112},{1,113},{2,114},{3,115},{4,116},{5,117},{6,118},{7,119},{8... | collective-permute-start | bytes 798728 | tf_op jit(solution)/shard_map/ppermute | solution.py:444
  10.6 19.5 %collective-permute-start = (f32[2,760,128]{2,1,0:T(8,128)S(1)}, f32[2,760,128]{2,1,0:T(8,128)S(1)}, u32[]{:S(2)}, u32[]{:S(2)}) collective-permute-start(f32[2,760,128]{2,1,0:T(8,128)S(1)} %get-tuple-element.15), channel_id=1, source_target_pairs={{0,15},{1,0},{2,1},{3,2},{4,3},{5,4},{6,5},{7,6},{8,7},{9,8},{10,9... | collective-permute-start | bytes 2334728 | tf_op jit(solution)/shard_map/ppermute | solution.py:444
  11.8 19.2 %copy-start = (f32[512]{0:T(512)S(1)}, f32[512]{0:T(512)}, u32[]{:S(2)}) copy-start(f32[512]{0:T(512)} %refs_2_.3) | copy-start | bytes 6148
  11.8 19.2 %copy-start.1 = (f32[512]{0:T(512)S(1)}, f32[512]{0:T(512)}, u32[]{:S(2)}) copy-start(f32[512]{0:T(512)} %refs_3_.3) | copy-start | bytes 6148
  11.8 19.2 %copy-start.2 = (s32[240]{0:T(256)S(1)}, s32[240]{0:T(256)}, u32[]{:S(2)}) copy-start(s32[240]{0:T(256)} %refs_0_.5) | copy-start | bytes 2884
  30.1 0.9 %copy-start.3 = (f32[2,760,128]{2,1,0:T(8,128)}, f32[2,760,128]{2,1,0:T(8,128)S(1)}, u32[]{:S(2)}) copy-start(f32[2,760,128]{2,1,0:T(8,128)S(1)} %collective-permute-done.refs_2_) | copy-start | bytes 2334724
  54.1 18.8 %collective-permute-start.5 = (f32[2,40,128]{2,1,0:T(8,128)S(1)}, f32[2,40,128]{2,1,0:T(8,128)S(1)}, u32[]{:S(2)}, u32[]{:S(2)}) collective-permute-start(f32[2,40,128]{2,1,0:T(8,128)S(1)} %get-tuple-element.23), channel_id=1, source_target_pairs={{0,17},{1,18},{2,19},{3,20},{4,21},{5,22},{6,23},{7,24},{8,25},{9,... | collective-permute-start | bytes 122888 | tf_op jit(solution)/shard_map/ppermute | solution.py:444
  54.2 18.7 %collective-permute-start.4 = (f32[13,40,128]{2,1,0:T(8,128)S(1)}, f32[13,40,128]{2,1,0:T(8,128)S(1)}, u32[]{:S(2)}, u32[]{:S(2)}) collective-permute-start(f32[13,40,128]{2,1,0:T(8,128)S(1)} %get-tuple-element.22), channel_id=1, source_target_pairs={{0,16},{1,17},{2,18},{3,19},{4,20},{5,21},{6,22},{7,23},{8,24},{9,... | collective-permute-start | bytes 798728 | tf_op jit(solution)/shard_map/ppermute | solution.py:444
  55.5 17.5 %collective-permute-start.3 = (f32[2,760,128]{2,1,0:T(8,128)S(1)}, f32[2,760,128]{2,1,0:T(8,128)S(1)}, u32[]{:S(2)}, u32[]{:S(2)}) collective-permute-start(f32[2,760,128]{2,1,0:T(8,128)S(1)} %get-tuple-element.21), channel_id=1, source_target_pairs={{0,1},{1,2},{2,3},{3,4},{4,5},{5,6},{6,7},{7,8},{8,9},{9,10},{10,1... | collective-permute-start | bytes 2334728 | tf_op jit(solution)/shard_map/ppermute | solution.py:444
